TPU v7x, 32 devices: a whole 2x2x4 slice. The times are simulated.
32 devices in a mesh: blk: 4 (over y, x), dom: 8 (over z, core).
Axes of the slice: x: 2, y: 2, z: 4, core: 2. Of those that a mesh axis runs over, the one named last changes fastest.
Arguments:
- cell_features: bfloat16 [8, 1024, 768], P('dom', 'blk'), may hold values from -6 to 6
- cotangent: bfloat16 [8, 1024, 768], P('dom', 'blk'), may hold values from -6 to 6
- query_weight: bfloat16 [768, 768], replicated
- key_weight: bfloat16 [768, 768], replicated
- value_weight: bfloat16 [768, 768], replicated, may hold values from -0.21875 to 0.21875
- out_weight: bfloat16 [768, 768], replicated, may hold values from -0.21875 to 0.21875
- anchor_index: int32 [8, 128], P('dom', 'blk'), may hold values from 0 to 255, as said below
- face_cells: int32 [8, 4, 2, 128], P('dom', 'blk'), may hold values from 0 to 255, as said below
- halo_count: int32 [8, 4, 2], P('dom', 'blk'), may hold values from 0 to 128, as said below
- neighbour_blocks: int32 [8, 8, 3], P('dom', 'blk'), may hold values from 0 to 3, as said below
Outputs:
- mixed: bfloat16 [8, 1024, 768], P('dom', 'blk')
- cell_grad: bfloat16 [8, 1024, 768], P('dom', 'blk')
- weight_grads: float32 [3072, 768], P(('blk', 'dom'))
Inputs may be any that keep to these rules, and one draw needn't show every extreme that they name: `anchor_index`: the 32 entries of one slot are different cells of that slot. `face_cells`: the 256 entries of one slot are different cells of that slot. halo_count[0, b, 0] and halo_count[7, b, 1] are 0 for every b; all other entries are 1 or more. `neighbour_blocks`: row b*2+j lists 3 different pool blocks, the first of them j itself.
All inputs are finite; a program needn't handle non-finite values.
Results may differ from a plain program's by a relative error of at most 0.017.
The roundings to bfloat16 on the way count: a program that leaves them out, or rounds other values in their place, can miss the bound.
Values may be sent and summed in bfloat16 or wider, within the bound.
A program may use at most 128 MiB of HBM per device.

v0:
```python
import math

import jax
import jax.numpy as jnp
from jax import lax
from jax.sharding import PartitionSpec as P

HEADS = 12
BS = 128
NB = 3


EPSILON = 1e-06
MASKED = -1e30


def extended_2(block, sides, width):
    for axis, dim in sides:
        count = lax.axis_size(axis)
        forward = [(i, i + 1) for i in range(count - 1)]
        backward = [(target, source) for source, target in forward]
        low = lax.ppermute(
            lax.slice_in_dim(block, block.shape[dim] - width, None, axis=dim), axis, forward
        )
        high = lax.ppermute(lax.slice_in_dim(block, 0, width, axis=dim), axis, backward)
        block = jnp.concatenate([low, block, high], axis=dim)
    return block


def split_heads(tensor):
    leading = tensor.shape[:-2]
    length = tensor.shape[-2]
    tensor = tensor.reshape(leading + (length, HEADS, tensor.shape[-1] // HEADS))
    return jnp.moveaxis(tensor, -2, -3)


def join_heads(tensor):
    tensor = jnp.moveaxis(tensor, -3, -2)
    return tensor.reshape(tensor.shape[:-2] + (tensor.shape[-2] * tensor.shape[-1],))


def attend(queries, key_rows, value_rows, upstream, validity):
    scaling = 1.0 / math.sqrt(queries.shape[-1])
    scores = (
        jnp.einsum("...qe,...ke->...qk", queries, key_rows, preferred_element_type=jnp.float32)
        * scaling
    )
    scores = jnp.where(validity[..., None, :], scores, MASKED)
    highest = jnp.max(scores, axis=-1, keepdims=True)
    powers = jnp.exp(scores - highest)
    probability = powers / jnp.sum(powers, axis=-1, keepdims=True)
    prob_rounded = probability.astype(jnp.bfloat16)
    out_rows = jnp.einsum(
        "...qk,...ke->...qe", prob_rounded, value_rows, preferred_element_type=jnp.float32
    )
    prob_grad = jnp.einsum(
        "...qe,...ke->...qk", upstream, value_rows, preferred_element_type=jnp.float32
    )
    score_grad = probability * (
        prob_grad - jnp.sum(probability * prob_grad, axis=-1, keepdims=True)
    )
    score_rounded = score_grad.astype(jnp.bfloat16)
    query_term = (
        jnp.einsum(
            "...qk,...ke->...qe", score_rounded, key_rows, preferred_element_type=jnp.float32
        )
        * scaling
    )
    key_term = (
        jnp.einsum("...qk,...qe->...ke", score_rounded, queries, preferred_element_type=jnp.float32)
        * scaling
    )
    value_term = jnp.einsum(
        "...qk,...qe->...ke", prob_rounded, upstream, preferred_element_type=jnp.float32
    )
    return (out_rows, query_term, key_term, value_term)


def body(
    cell_features,
    cotangent,
    query_weight,
    key_weight,
    value_weight,
    out_weight,
    anchor_index,
    face_cells,
    halo_count,
    neighbour_blocks,
):
    x_local = cell_features[0]
    dy_local = cotangent[0]
    cell_count, width = x_local.shape
    block_count = cell_count // BS
    as_float = x_local.astype(jnp.float32)
    inverse = lax.rsqrt(jnp.mean(as_float * as_float, axis=-1, keepdims=True) + EPSILON)
    normed = (as_float * inverse).astype(jnp.bfloat16)
    w_merged = jnp.concatenate([query_weight, key_weight, value_weight], axis=1)
    projected = jnp.dot(normed, w_merged, preferred_element_type=jnp.float32).astype(jnp.bfloat16)
    queries = projected[:, :width]
    keyval_local = projected[:, width:]
    grad_mid = jnp.dot(dy_local, out_weight.T, preferred_element_type=jnp.float32).astype(
        jnp.bfloat16
    )
    anchor_rows = anchor_index[0]
    anchors = lax.all_gather(keyval_local[anchor_rows], "blk", axis=0, tiled=True)
    face_rows = face_cells[0, 0].reshape(2 * BS)
    live_count = halo_count[0, 0]
    extended = extended_2(keyval_local[face_rows], (("dom", 0),), BS)
    halo_keyval = jnp.concatenate([extended[:BS], extended[3 * BS :]], 0)
    key_pool = jnp.concatenate([keyval_local, halo_keyval], 0).reshape(
        block_count + 2, BS, 2 * width
    )
    positions = jnp.arange(BS)
    live_rows = jnp.concatenate(
        [
            jnp.ones((block_count, BS), bool),
            (positions < live_count[0])[None],
            (positions < live_count[1])[None],
        ],
        0,
    )
    near_index = neighbour_blocks[0]
    chosen = key_pool[near_index].reshape(block_count, NB * BS, 2 * width)
    chosen_live = live_rows[near_index].reshape(block_count, 1, NB * BS)
    all_live = jnp.ones((anchors.shape[0],), bool)

    def head_pass(members):
        return attend(members[0], members[1], members[2], members[3], all_live)

    anchor_out, anchor_dquery, anchor_dkey, anchor_dvalue = lax.map(
        head_pass,
        (
            split_heads(queries),
            split_heads(anchors[:, :width]),
            split_heads(anchors[:, width:]),
            split_heads(grad_mid),
        ),
    )
    near_out, near_dquery, near_dkey, near_dvalue = attend(
        split_heads(queries.reshape(block_count, BS, width)),
        split_heads(chosen[..., :width]),
        split_heads(chosen[..., width:]),
        split_heads(grad_mid.reshape(block_count, BS, width)),
        chosen_live,
    )
    attended = (join_heads(anchor_out) + join_heads(near_out).reshape(cell_count, width)).astype(
        jnp.bfloat16
    )
    query_grad = (
        join_heads(anchor_dquery) + join_heads(near_dquery).reshape(cell_count, width)
    ).astype(jnp.bfloat16)
    chosen_grad = jnp.concatenate([join_heads(near_dkey), join_heads(near_dvalue)], -1)
    chosen_grad = chosen_grad.reshape(block_count * NB, BS, 2 * width)
    onehot = (near_index.reshape(-1)[:, None] == jnp.arange(block_count + 2)[None, :]).astype(
        jnp.float32
    )
    pool_grad = jnp.einsum("sp,sbf->pbf", onehot, chosen_grad, precision=lax.Precision.HIGHEST)
    anchor_term = jnp.concatenate([join_heads(anchor_dkey), join_heads(anchor_dvalue)], -1)
    anchor_term = lax.optimization_barrier(anchor_term.astype(jnp.bfloat16)).astype(jnp.float32)
    anchor_share = lax.psum_scatter(
        anchor_term.astype(jnp.bfloat16), "blk", scatter_dimension=0, tiled=True
    ).astype(jnp.float32)
    halo_grad = pool_grad[block_count:].reshape(2 * BS, 2 * width).astype(jnp.bfloat16)
    returned = extended_2(halo_grad, (("dom", 0),), BS)
    came_back = jnp.concatenate([returned[:BS], returned[3 * BS :]], 0).astype(jnp.float32)
    keyval_grad = pool_grad[:block_count].reshape(cell_count, 2 * width)
    keyval_grad = keyval_grad.at[jnp.concatenate([anchor_rows, face_rows])].add(
        jnp.concatenate([anchor_share, came_back], 0)
    )
    proj_grads = jnp.concatenate([query_grad, keyval_grad.astype(jnp.bfloat16)], 1)
    inner_term = jnp.dot(normed.T, proj_grads, preferred_element_type=jnp.float32)
    inner_term = inner_term.reshape(width, 3, width).transpose(1, 0, 2).reshape(3 * width, width)
    out_term = jnp.dot(attended.T, dy_local, preferred_element_type=jnp.float32)
    weight_term = jnp.concatenate([inner_term, out_term], 0)
    weight_grads = lax.psum_scatter(weight_term, ("blk", "dom"), scatter_dimension=0, tiled=True)
    normed_grad = jnp.dot(proj_grads, w_merged.T, preferred_element_type=jnp.float32)
    cot_float = dy_local.astype(jnp.float32)
    cube = inverse * inverse * inverse
    cell_grad = (
        cot_float
        + inverse * normed_grad
        - as_float * cube * jnp.mean(normed_grad * as_float, axis=-1, keepdims=True)
    )
    mixed = as_float + jnp.dot(attended, out_weight, preferred_element_type=jnp.float32)
    return (mixed.astype(jnp.bfloat16)[None], cell_grad.astype(jnp.bfloat16)[None], weight_grads)


def solution(mesh):
    return jax.shard_map(
        body,
        mesh=mesh,
        in_specs=(
            P("dom", "blk", None),
            P("dom", "blk", None),
            P(),
            P(),
            P(),
            P(),
            P("dom", "blk"),
            P("dom", "blk", None, None),
            P("dom", "blk", None),
            P("dom", "blk", None),
        ),
        out_specs=(P("dom", "blk", None), P("dom", "blk", None), P(("blk", "dom"), None)),
        check_vma=False,
    )
```

profile of v0, /device:TPU:10, one launch (start us, length us, event | category | flops | bytes accessed | tf_op | source)
XLA Modules:
  0.0 359.5 jit_solution(11480108179254011056)
XLA Ops:
  7.3 1.5 constant_dynamic-update-slice_fusion.2
  14.5 2.0 collective-permute-start.1
  16.5 2.4 collective-permute-start
  18.9 1.8 slice.74
  23.1 10.3 %all-gather = bf16[128,1536]{1,0:T(8,128)(2,1)S(1)} all-gather(bf16[32,1536]{1,0:T(8,128)(2,1)} %gather_fusion), channel_id=2, replica_groups=mesh['blk'=4,'dom'=8] {'blk'}, dimensions={0}, use_global_device_ids=true | all-gather | bytes 491520 | tf_op jit(solution)/shard_map/all_gather | solution.py:106
  34.2 1.7 copy.83
  35.9 1.7 copy.84
  40.1 70.5 %while.16 = (s32[]{:T(128)}, f32[12,256,64]{1,2,0:T(8,128)S(1)}, f32[12,256,64]{1,2,0:T(8,128)}, bf16[12,128,64]{1,2,0:T(8,128)(2,1)}, bf16[12,128,64]{1,2,0:T(8...) while((s32[]{:T(128)}, f32[12,256,64]{1,2,0:T(8,128)S(1)}, ...), condition=%wide.region_5.6_spmd, body=%wide.region_1.5_spmd.sunk | while | flops 25812224 | bytes 1657965 | solution.py:131
  43.0 1.5 fusion.148
  48.9 1.5 fusion.148
  54.8 1.5 fusion.148
  60.6 1.5 fusion.148
  66.5 1.5 fusion.148
  72.4 1.5 fusion.148
  78.3 1.5 fusion.148
  84.1 1.5 fusion.148
  90.0 1.5 fusion.148
  95.9 1.5 fusion.148
  101.8 1.5 fusion.148
  107.6 1.5 fusion.148
  110.7 2.1 pad_maximum_fusion.4
  112.8 1.9 copy.112
  116.0 1.8 iota_compare_fusion.1
  122.1 2.3 copy.98
  127.0 2.2 gather_fusion.3
  129.2 2.8 fusion.100
  133.5 1.7 copy.120
  136.0 1.7 fusion.105
  137.7 2.1 fusion.50
  140.7 1.6 multiply_reduce_fusion.1
  143.4 2.1 multiply_bitcast_fusion
  145.4 2.1 fusion.46
  147.5 3.3 copy.102
  150.7 4.7 %concatenate.61 = f32[6,128,768]{1,0,2:T(8,128)} reshape(f32[2,384,12,64]{1,0,3,2:T(2,128)} %copy.102) | data formatting | bytes 4718592 | tf_op jit(solution)/shard_map/concatenate | solution.py:153
  155.5 3.6 %copy.104 = f32[6,128,768]{2,0,1:T(8,128)} copy(f32[6,128,768]{1,0,2:T(8,128)} %concatenate.61) | data formatting | bytes 4718592 | tf_op jit(solution)/shard_map/concatenate | solution.py:153
  159.1 4.9 %copy.100 = f32[2,384,12,64]{1,0,3,2:T(2,128)} copy(f32[2,384,12,64]{1,3,2,0:T(8,128)} %multiply_bitcast_fusion) | data formatting | bytes 4718592 | tf_op jit(solution)/shard_map/mul | solution.py:70
  164.1 4.7 %concatenate.60 = f32[6,128,768]{1,0,2:T(8,128)} reshape(f32[2,384,12,64]{1,0,3,2:T(2,128)} %copy.100) | data formatting | bytes 4718592 | tf_op jit(solution)/shard_map/concatenate | solution.py:153
  168.8 3.6 %copy.103 = f32[6,128,768]{2,0,1:T(8,128)} copy(f32[6,128,768]{1,0,2:T(8,128)} %concatenate.60) | data formatting | bytes 4718592 | tf_op jit(solution)/shard_map/concatenate | solution.py:153
  172.5 8.1 %fusion.106 = (bf16[4,128,1536]{2,0,1:T(4,128)(2,1)S(1)}, f32[4,128,1536]{2,0,1:T(4,128)}) fusion(f32[6,128,768]{2,0,1:T(8,128)} %copy.104, f32[6,128,768]{2,0,1:T(8,128)} %copy.103, s32[6]{0:T(128)S(1)} %copy-done.27), kind=kOutput, calls=%fused_computation.154 | convolution fusion | flops 58589208 | bytes 9437208 | tf_op jit(solution)/shard_map/sp,sbf->pbf/dot_general | solution.py:158
  182.8 1.9 collective-permute-start.3
  185.6 2.4 collective-permute-start.2
  188.9 2.1 add_convert_fusion
  193.8 1.9 fusion.80
  195.7 4.9 %scatter_custom_fusion = f32[256,1536]{1,0:T(8,128)S(1)} fusion(f32[256,1536]{1,0:T(8,128)S(1)} %bitcast.251, s32[288]{0:T(512)} %fusion.92, bf16[128,1536]{1,0:T(8,128)(2,1)} %collective-permute-done.3, bf16[]{:T(256)} %constant.67, bf16[128,1536]{1,0:T(8,128)(2,1)} %collective-permute-done.2, bf16[32,1536]{1,0:T(8,128)(2,1)} %reduce-scatter.7.cloned.1.call-done), kind=kCustom, calls=%fused_computation.63 | custom fusion | flops 3096576 | bytes 2458112 | tf_op jit(solution)/shard_map/scatter-add | solution.py:168
  201.8 1.4 copy.107
  203.2 5.5 %fusion.73 = f32[768,3,768]{2,0,1:T(8,128)} fusion(bf16[3,768,256]{2,1,0:T(8,128)(2,1)} %bitcast.252, bf16[1,256,768]{2,1,0:T(8,128)(2,1)S(1)} %copy-done.4, f32[256]{0:T(256)S(1)} %get-tuple-element.115), kind=kOutput, calls=%fused_computation.104 | convolution fusion | flops 906559488 | bytes 8651776 | tf_op jit(solution)/shard_map/dot_general | solution.py:172
  208.7 7.3 %pad_maximum_fusion = f32[3072,768]{1,0:T(8,128)} fusion(f32[768,768]{1,0:T(8,128)S(1)} %copy-done.1, f32[2304,768]{1,0:T(8,128)} %bitcast.246), kind=kLoop, calls=%fused_computation.47 | loop fusion | flops 2359296 | bytes 18874368 | tf_op jit(solution)/shard_map/concatenate | solution.py:175
  221.9 130.8 %reduce-scatter.5.cloned.1.call-done = f32[96,768]{1,0:T(8,128)} async-done(((f32[3072,768]{1,0:T(8,128)}), f32[96,768]{1,0:T(8,128)}) %reduce-scatter.5.cloned.1.call-update) | async-done | bytes 294928 | tf_op jit(solution)/shard_map/reduce_scatter | solution.py:176
  (206 shorter events, 89.7 us)
Async XLA Ops:
  7.2 30.5 %copy-start = (bf16[768,768]{1,0:T(8,128)(2,1)S(1)}, bf16[768,768]{1,0:T(8,128)(2,1)}, u32[]{:S(2)}) copy-start(bf16[768,768]{1,0:T(8,128)(2,1)} %param.17) | copy-start | bytes 3538948
  7.2 1.6 copy-start.3
  7.2 1.8 copy-start.18
  7.2 188.5 %reduce-scatter.7.cloned.1.call-start = ((), (), s32[]{:S(2)}) async-start(), calls=%async_computation.3 | async-start | bytes 491520 | tf_op jit(solution)/shard_map/reduce_scatter | solution.py:161
  7.2 2.1 copy-start.19
  9.5 1.7 copy-start.22
  9.5 1.8 copy-start.24
  9.5 1.8 copy-start.28
  11.2 1.1 copy-start.17
  14.5 23.2 %copy-start.6 = (bf16[1,256,768]{2,1,0:T(8,128)(2,1)S(1)}, bf16[1,256,768]{2,1,0:T(8,128)(2,1)}, u32[]{:S(2)}) copy-start(bf16[1,256,768]{2,1,0:T(8,128)(2,1)} %param.13) | copy-start | bytes 1179652
  14.5 111.3 %collective-permute-start.1 = (bf16[128,1536]{1,0:T(8,128)(2,1)}, bf16[128,1536]{1,0:T(8,128)(2,1)}, u32[]{:S(2)}, u32[]{:S(2)}) collective-permute-start(bf16[128,1536]{1,0:T(8,128)(2,1)} %get-tuple-element.111), channel_id=1, source_target_pairs={{1,0},{2,1},{3,2},{4,3},{5,4},{6,5},{7,6},{9,8},{10,9},{11,10},{12... | collective-permute-start | bytes 1179656 | tf_op jit(solution)/shard_map/ppermute | solution.py:25
  16.5 109.3 %collective-permute-start = (bf16[128,1536]{1,0:T(8,128)(2,1)}, bf16[128,1536]{1,0:T(8,128)(2,1)}, u32[]{:S(2)}, u32[]{:S(2)}) collective-permute-start(bf16[128,1536]{1,0:T(8,128)(2,1)} %get-tuple-element.110), channel_id=1, source_target_pairs={{0,1},{1,2},{2,3},{3,4},{4,5},{5,6},{6,7},{8,9},{9,10},{10,11},{11... | collective-permute-start | bytes 1179656 | tf_op jit(solution)/shard_map/ppermute | solution.py:22
  40.1 74.6 %copy-start.26 = (s32[1,2,3]{2,1,0:T(2,128)S(1)}, s32[1,2,3]{2,1,0:T(2,128)}, u32[]{:S(2)}) copy-start(s32[1,2,3]{2,1,0:T(2,128)} %param.21) | copy-start | bytes 76
  40.1 75.2 %copy-start.25 = (s32[1,1,2]{2,1,0:T(1,128)S(1)}, s32[1,1,2]{2,1,0:T(1,128)}, u32[]{:S(2)}) copy-start(s32[1,1,2]{2,1,0:T(1,128)} %param.20) | copy-start | bytes 28
  110.7 13.7 %copy-start.10 = (f32[12,256,64]{1,2,0:T(8,128)}, f32[12,256,64]{1,2,0:T(8,128)S(1)}, u32[]{:S(2)}) copy-start(f32[12,256,64]{1,2,0:T(8,128)S(1)} %get-tuple-element.53) | copy-start | bytes 2359300
  114.7 238.0 %reduce-scatter.5.cloned.1.call-start = ((), (), s32[]{:S(2)}) async-start(), calls=%async_computation.2 | async-start | bytes 9732096 | tf_op jit(solution)/shard_map/reduce_scatter | solution.py:176
  132.0 3.1 copy-start.5
  136.0 1.7 copy-start.20
  137.7 2.1 copy-start.21
  168.8 3.7 %copy-start.27 = (s32[6]{0:T(128)S(1)}, s32[6]{0:T(128)}, u32[]{:S(2)}) copy-start(s32[6]{0:T(128)} %eq.15) | copy-start | bytes 76
  180.6 7.3 %copy-start.14 = (f32[2,128,12,64]{1,3,2,0:T(8,128)S(1)}, f32[2,128,12,64]{1,3,2,0:T(8,128)}, u32[]{:S(2)}) copy-start(f32[2,128,12,64]{1,3,2,0:T(8,128)} %fusion.46) | copy-start | bytes 2359300
  182.8 12.9 %collective-permute-start.3 = (bf16[128,1536]{1,0:T(8,128)(2,1)}, bf16[128,1536]{1,0:T(8,128)(2,1)}, u32[]{:S(2)}, u32[]{:S(2)}) collective-permute-start(bf16[128,1536]{1,0:T(8,128)(2,1)} %bitcast.216), channel_id=1, source_target_pairs={{1,0},{2,1},{3,2},{4,3},{5,4},{6,5},{7,6},{9,8},{10,9},{11,10},{12... | collective-permute-start | bytes 1179656 | tf_op jit(solution)/shard_map/ppermute | solution.py:25
  185.6 10.2 %collective-permute-start.2 = (bf16[128,1536]{1,0:T(8,128)(2,1)}, bf16[128,1536]{1,0:T(8,128)(2,1)}, u32[]{:S(2)}, u32[]{:S(2)}) collective-permute-start(bf16[128,1536]{1,0:T(8,128)(2,1)} %bitcast.217), channel_id=1, source_target_pairs={{0,1},{1,2},{2,3},{3,4},{4,5},{5,6},{6,7},{8,9},{9,10},{10,11},{11... | collective-permute-start | bytes 1179656 | tf_op jit(solution)/shard_map/ppermute | solution.py:22
  188.6 2.5 copy-start.8
  188.9 3.3 copy-start.2
  192.8 1.0 copy-start.7
  200.7 1.0 copy-start.15
  200.8 0.9 copy-start.12
  201.7 1.5 copy-start.4
  203.2 5.5 %copy-start.1 = (f32[768,768]{1,0:T(8,128)S(1)}, f32[768,768]{1,0:T(8,128)}, u32[]{:S(2)}) copy-start(f32[768,768]{1,0:T(8,128)} %fusion.80) | copy-start | bytes 7077892
  216.0 1.1 copy-start.9
  216.0 1.8 copy-start.11
  217.1 2.1 copy-start.23
  217.7 1.7 copy-start.13
  217.7 1.9 copy-start.16
Sparse Core Ops, SparseCore 0:
  114.8 24.8 reduce-scatter.6
  216.1 136.5 reduce-scatter.4
where the time goes:
time: 366 us; the launch traced here: 360 us
  waiting for transfers between devices  131 us (36%)
  matrix products  99.2 us (27%)
  local copies, waits for them, and re-layouts  67.1 us (18%)
  other arithmetic  28.5 us (8%)
  between operations  14.5 us (4%)
  blocking collectives  10.3 us (3%)
  starting transfers between devices  8.83 us (2%)
    reduce_scatter x1, waiting for transfers between devices, body(): lax.psum_scatter(weight_term, ('blk', 'dom'), scatter_dimension=0, tiled=...  131 us
    dot_general x13, matrix products, attend(): jnp.einsum('...qk,...ke->...qe', score_rounded, key_rows, preferred_eleme...  20 us
    concatenate x4, local copies, waits for them, and re-layouts, body(): jnp.concatenate([join_heads(near_dkey), join_heads(near_dvalue)], -1)  16.8 us
    unnamed x66, local copies, waits for them, and re-layouts  13.4 us
    dot_general x13, matrix products, attend(): jnp.einsum('...qe,...ke->...qk', upstream, value_rows, preferred_element_...  13 us
    dot_general x13, matrix products, attend(): jnp.einsum('...qk,...ke->...qe', prob_rounded, value_rows, preferred_elem...  12.5 us
    dot_general x13, matrix products, attend(): jnp.einsum('...qe,...ke->...qk', queries, key_rows, preferred_element_typ...  12.1 us
    dot_general x13, matrix products, attend(): jnp.einsum('...qk,...qe->...ke', score_rounded, queries, preferred_elemen...  11.2 us
  transfers between devices with their start and end apart: 6, of which 1 were waited for; matrix products, arithmetic and copies ran while one was open for 46% of the time, Pallas kernels for 0%

commit v1 on v0

v1 whole, which is shorter than its diff:
```python
import functools

import jax
import jax.numpy as jnp
from jax import lax
from jax.experimental import pallas as pl
from jax.experimental.pallas import tpu as pltpu
from jax.sharding import PartitionSpec as P

HEAD = 64
PAIR = 2 * HEAD
BS = 128
EPSILON = 1e-06
MASKED = -1e30
SCALING = 0.125
MESH = pl.DeviceIdType.MESH
F32 = jnp.float32
BF16 = jnp.bfloat16


def mm(a, b):
    return lax.dot_general(a, b, (((1,), (0,)), ((), ())), preferred_element_type=F32)


def mm_nt(a, b):
    return lax.dot_general(a, b, (((1,), (1,)), ((), ())), preferred_element_type=F32)


def mm_tn(a, b):
    return lax.dot_general(a, b, (((0,), (0,)), ((), ())), preferred_element_type=F32)


def attend(q2, g2, keys, values, live):
    scores = mm_nt(q2, keys)
    if live is not None:
        scores = jnp.where(jnp.broadcast_to(live, scores.shape) > 0, scores, MASKED)
    powers = jnp.exp(scores - jnp.max(scores, axis=-1, keepdims=True))
    prob = powers * (1.0 / jnp.sum(powers, axis=-1, keepdims=True))
    prob_b = prob.astype(BF16)
    out = mm(prob_b, values)
    prob_grad = mm_nt(g2, values)
    score_grad = prob * (prob_grad - jnp.sum(prob * prob_grad, axis=-1, keepdims=True))
    score_b = score_grad.astype(BF16)
    query_term = mm(score_b, keys) * SCALING
    key_term = mm_tn(score_b, q2)
    value_term = mm_tn(prob_b, g2)
    return out, query_term, key_term, value_term


def kernel(
    n_blk,
    n_dom,
    x_ref,
    dy_ref,
    wq_ref,
    wk_ref,
    wv_ref,
    wo_ref,
    idx_ref,
    count_ref,
    near_ref,
    mixed_ref,
    cgrad_ref,
    wgrad_ref,
    normed,
    q_s,
    g_s,
    kv_s,
    hot_s,
    faces,
    anchors,
    halo,
    ag_out,
    ag_in,
    hg_out,
    hg_in,
    near_s,
    att_f,
    qg_f,
    att_b,
    grads,
    lhs,
    rhs,
    wsum,
    wpart,
    from_left,
    from_right,
    anc_send,
    anc_recv,
    face_send,
    face_recv,
    lhs_send,
    lhs_recv,
    rhs_send,
    rhs_recv,
    ag_send,
    ag_recv,
    hg_send,
    hg_recv,
    core_sem,
    right_send,
    right_recv,
    left_send,
    left_recv,
):
    cells, width = x_ref.shape
    rows = lhs.shape[2]
    share = wsum.shape[2]
    chips = n_dom // 2
    pairs = width // PAIR
    blk = lax.axis_index("blk")
    dom = lax.axis_index("dom")
    chip = dom // 2
    core = dom - 2 * chip
    mate = dom + 1 - 2 * core

    def copy(src, dst, send, recv, target):
        return pltpu.make_async_remote_copy(
            src_ref=src,
            dst_ref=dst,
            send_sem=send,
            recv_sem=recv,
            device_id=target,
            device_id_type=MESH,
        )

    def each_peer(action):
        for j in range(n_blk):
            pl.when(blk != j)(functools.partial(action, j))

    barrier = pltpu.get_barrier_semaphore()
    steps = (-2, -1, 1, 2)

    def greet(target):
        pl.semaphore_signal(barrier, inc=1, device_id=target, device_id_type=MESH)

    each_peer(lambda j: greet({"blk": j}))
    for step in steps:
        there = (dom + step >= 0) & (dom + step < n_dom)
        pl.when(there)(functools.partial(lambda s: greet({"dom": dom + s}), step))

    x = x_ref[...].astype(F32)
    inverse = lax.rsqrt(jnp.mean(x * x, axis=-1, keepdims=True) + EPSILON)
    normed[...] = (x * inverse).astype(BF16)
    kv_s[:, :width] = mm(normed[...], wk_ref[...]).astype(BF16)
    kv_s[:, width:] = mm(normed[...], wv_ref[...]).astype(BF16)

    spots = lax.broadcasted_iota(jnp.int32, hot_s.shape, 0)
    hot_s[...] = jnp.where(spots == idx_ref[...], 1.0, 0.0).astype(BF16)
    picked = 2 * BS + anchors.shape[1]
    for part in range(2):
        columns = slice(part * width, (part + 1) * width)
        chosen = mm_tn(hot_s[:, : 3 * BS], kv_s[:, columns]).astype(BF16)
        faces[0, :, columns] = chosen[:BS]
        faces[1, :, columns] = chosen[BS : 2 * BS]
        anchors[blk, :, columns] = chosen[2 * BS : picked]

    expected = n_blk - 1
    for step in steps:
        there = (dom + step >= 0) & (dom + step < n_dom)
        expected = expected + jnp.where(there, 1, 0)
    pl.semaphore_wait(barrier, expected)

    has_low = dom > 0
    has_high = dom < n_dom - 1

    def anchor_copy(j):
        return copy(
            anchors.at[blk], anchors.at[blk], anc_send.at[j], anc_recv.at[blk], {"blk": j}
        )

    def anchor_arrival(j):
        return copy(anchors.at[j], anchors.at[j], anc_send.at[j], anc_recv.at[j], {"blk": j})

    def face_copy(side):
        step = 2 * side - 1
        return copy(
            faces.at[side],
            halo.at[1 - side],
            face_send.at[side],
            face_recv.at[1 - side],
            {"dom": dom + step},
        )

    def weight_of(j):
        return (j * rows) // width, (j * rows) % width

    def lhs_copy(j):
        weight, start = weight_of(j)
        source = normed if weight < 3 else att_b
        return copy(
            source.at[:, start : start + rows],
            lhs.at[blk],
            lhs_send.at[j],
            lhs_recv.at[blk],
            {"blk": j},
        )

    def rhs_copy(j):
        weight, _ = weight_of(j)
        source = grads.at[weight] if weight < 3 else dy_ref
        return copy(source, rhs.at[blk], rhs_send.at[j], rhs_recv.at[blk], {"blk": j})

    def lhs_own(j):
        weight, start = weight_of(j)
        source = normed if weight < 3 else att_b
        lhs[j] = source[:, start : start + rows]

    def rhs_own(j):
        weight, _ = weight_of(j)
        rhs[j] = grads[weight] if weight < 3 else dy_ref[...]

    def send_lhs(wanted):
        for j in range(n_blk):
            if weight_of(j)[0] in wanted:
                pl.when(blk != j)(functools.partial(lambda k: lhs_copy(k).start(), j))
                pl.when(blk == j)(functools.partial(lhs_own, j))

    def send_rhs(wanted):
        for j in range(n_blk):
            if weight_of(j)[0] in wanted:
                pl.when(blk != j)(functools.partial(lambda k: rhs_copy(k).start(), j))
                pl.when(blk == j)(functools.partial(rhs_own, j))

    each_peer(lambda j: anchor_copy(j).start())
    pl.when(has_low)(lambda: face_copy(0).start())
    pl.when(has_high)(lambda: face_copy(1).start())
    send_lhs((0, 1, 2))
    send_rhs((3,))

    q_s[...] = mm(normed[...], wq_ref[...]).astype(BF16)
    g_s[...] = mm_nt(dy_ref[...], wo_ref[...]).astype(BF16)

    @pl.when(jnp.logical_not(has_low))
    def _():
        halo[0] = jnp.zeros(halo.shape[1:], BF16)
        hg_in[0] = jnp.zeros(hg_in.shape[1:], BF16)

    @pl.when(jnp.logical_not(has_high))
    def _():
        halo[1] = jnp.zeros(halo.shape[1:], BF16)
        hg_in[1] = jnp.zeros(hg_in.shape[1:], BF16)

    lane = lax.broadcasted_iota(jnp.int32, (1, PAIR), 1)
    first = jnp.where(lane < HEAD, 1.0, 0.0)
    first_b = first.astype(BF16)
    second_b = (1.0 - first).astype(BF16)

    def stacked(rows_of, scale):
        return jnp.concatenate([rows_of * (first_b * scale), rows_of * (second_b * scale)], 0)

    def unstacked(tensor):
        half = tensor.shape[0] // 2
        keep = jnp.broadcast_to(first, (half, PAIR)) > 0
        return jnp.where(keep, tensor[:half], tensor[half:])

    each_peer(lambda j: anchor_arrival(j).wait_recv())
    anchor_count = n_blk * anchors.shape[1]

    def anchor_pair(h, carry):
        sl = pl.ds(pl.multiple_of(h * PAIR, PAIR), PAIR)
        vsl = pl.ds(pl.multiple_of(width + h * PAIR, PAIR), PAIR)
        q2 = stacked(q_s[:, sl], SCALING)
        g2 = stacked(g_s[:, sl], 1.0)
        keys = anchors[:, :, sl].reshape(anchor_count, PAIR)
        values = anchors[:, :, vsl].reshape(anchor_count, PAIR)
        out, query_term, key_term, value_term = attend(q2, g2, keys, values, None)
        att_f[:, sl] = unstacked(out)
        qg_f[:, sl] = unstacked(query_term)
        ag_out[:, :, sl] = key_term.astype(BF16).reshape(n_blk, -1, PAIR)
        ag_out[:, :, vsl] = value_term.astype(BF16).reshape(n_blk, -1, PAIR)
        return carry

    lax.fori_loop(0, pairs, anchor_pair, 0)

    def ag_copy(j):
        return copy(ag_out.at[j], ag_in.at[blk], ag_send.at[j], ag_recv.at[blk], {"blk": j})

    def ag_arrival(j):
        return copy(ag_out.at[j], ag_in.at[j], ag_send.at[j], ag_recv.at[j], {"blk": j})

    each_peer(lambda j: ag_copy(j).start())
    ag_in[blk] = ag_out[blk]

    def face_arrival(side):
        step = 2 * side - 1
        return copy(
            faces.at[side],
            halo.at[side],
            face_send.at[side],
            face_recv.at[side],
            {"dom": dom + step},
        )

    pl.when(has_low)(lambda: face_arrival(0).wait_recv())
    pl.when(has_high)(lambda: face_arrival(1).wait_recv())

    blocks = cells // BS
    pool_rows = cells + 2 * BS
    spot = lax.broadcasted_iota(jnp.int32, (1, pool_rows), 1)
    zero = jnp.zeros((1, pool_rows), jnp.int32)
    one = zero + 1
    live_to = jnp.where(
        spot < cells, pool_rows, jnp.where(spot < cells + BS, cells, cells + BS)
    )
    live_to = live_to + jnp.where(
        spot < cells,
        0,
        jnp.where(spot < cells + BS, zero + count_ref[0, 0], zero + count_ref[0, 1]),
    )
    alive = jnp.where(spot < live_to, one, zero)
    live = []
    for j in range(blocks):
        listed = zero
        for i in range(near_ref.shape[1]):
            low = near_ref[j, i] * BS
            inside = jnp.where(spot >= low, one, zero) * jnp.where(spot < low + BS, one, zero)
            listed = listed + inside
        live.append((listed * alive).astype(F32))

    def near_pair(h, carry):
        sl = pl.ds(pl.multiple_of(h * PAIR, PAIR), PAIR)
        vsl = pl.ds(pl.multiple_of(width + h * PAIR, PAIR), PAIR)
        keys = jnp.concatenate([kv_s[:, sl], halo[0, :, sl], halo[1, :, sl]], 0)
        values = jnp.concatenate([kv_s[:, vsl], halo[0, :, vsl], halo[1, :, vsl]], 0)
        key_sum = value_sum = None
        for j in range(blocks):
            own = slice(j * BS, (j + 1) * BS)
            q2 = stacked(q_s[own, sl], SCALING)
            g2 = stacked(g_s[own, sl], 1.0)
            out, query_term, key_term, value_term = attend(q2, g2, keys, values, live[j])
            att_f[own, sl] += unstacked(out)
            qg_f[own, sl] += unstacked(query_term)
            key_sum = key_term if key_sum is None else key_sum + key_term
            value_sum = value_term if value_sum is None else value_sum + value_term
        near_s[:, sl] = key_sum[:cells]
        near_s[:, vsl] = value_sum[:cells]
        for side in range(2):
            part = slice(cells + side * BS, cells + (side + 1) * BS)
            hg_out[side, :, sl] = key_sum[part].astype(BF16)
            hg_out[side, :, vsl] = value_sum[part].astype(BF16)
        return carry

    lax.fori_loop(0, pairs, near_pair, 0)

    def hg_copy(side):
        step = 2 * side - 1
        return copy(
            hg_out.at[side],
            hg_in.at[1 - side],
            hg_send.at[side],
            hg_recv.at[1 - side],
            {"dom": dom + step},
        )

    def hg_arrival(side):
        step = 2 * side - 1
        return copy(
            hg_out.at[side],
            hg_in.at[side],
            hg_send.at[side],
            hg_recv.at[side],
            {"dom": dom + step},
        )

    pl.when(has_low)(lambda: hg_copy(0).start())
    pl.when(has_high)(lambda: hg_copy(1).start())
    att_b[...] = att_f[...].astype(BF16)
    grads[0] = qg_f[...].astype(BF16)
    send_lhs((3,))
    send_rhs((0,))

    each_peer(lambda j: ag_arrival(j).wait_recv())
    pl.when(has_low)(lambda: hg_arrival(0).wait_recv())
    pl.when(has_high)(lambda: hg_arrival(1).wait_recv())

    for part in (0, 1):
        columns = slice(part * width, (part + 1) * width)
        came = jnp.concatenate(
            [
                hg_in[0, :, columns],
                hg_in[1, :, columns],
                ag_in[:, :, columns].reshape(anchor_count, width),
            ],
            0,
        )
        grads[1 + part] = (near_s[:, columns] + mm(hot_s[...], came)).astype(BF16)
        send_rhs((1 + part,))

    mixed_ref[...] = (x_ref[...].astype(F32) + mm(att_b[...], wo_ref[...])).astype(BF16)
    back = mm_nt(grads[0], wq_ref[...]) + mm_nt(grads[1], wk_ref[...])
    back = back + mm_nt(grads[2], wv_ref[...])
    x = x_ref[...].astype(F32)
    inverse = lax.rsqrt(jnp.mean(x * x, axis=-1, keepdims=True) + EPSILON)
    cube = inverse * inverse * inverse
    pull = jnp.mean(back * x, axis=-1, keepdims=True)
    cgrad_ref[...] = (dy_ref[...].astype(F32) + inverse * back - x * (cube * pull)).astype(BF16)

    def operand_arrivals(j):
        copy(lhs.at[j], lhs.at[j], lhs_send.at[j], lhs_recv.at[j], {"blk": j}).wait_recv()
        copy(rhs.at[j], rhs.at[j], rhs_send.at[j], rhs_recv.at[j], {"blk": j}).wait_recv()

    each_peer(operand_arrivals)
    left_all = lhs[...].reshape(n_blk * cells, rows)
    right_all = rhs[...].reshape(n_blk * cells, width)
    product = mm_tn(left_all, right_all)
    for d in range(n_dom):
        wsum[d % 2, d // 2] = product[d * share : (d + 1) * share]

    swap = copy(wsum.at[1 - core], wpart, core_sem.at[0], core_sem.at[1], {"dom": mate})
    swap.start()
    swap.wait_recv()
    wsum[core] += wpart[...]

    def right_copy(source, t):
        return copy(
            source, from_left.at[t], right_send.at[t], right_recv.at[t], {"dom": dom + 2}
        )

    def left_copy(source, t):
        return copy(
            source, from_right.at[t], left_send.at[t], left_recv.at[t], {"dom": dom - 2}
        )

    def right_arrival(t):
        return copy(
            from_left.at[t], from_left.at[t], right_send.at[t], right_recv.at[t], {"dom": dom - 2}
        )

    def left_arrival(t):
        return copy(
            from_right.at[t], from_right.at[t], left_send.at[t], left_recv.at[t], {"dom": dom + 2}
        )

    last = chips - 1
    for step in range(chips - 1):
        t_right = last - step + chip
        t_left = step - (last - chip)

        @pl.when(chip == 0)
        def _():
            right_copy(wsum.at[core, t_right], t_right).start()

        @pl.when((chip > 0) & (chip <= step))
        def _():
            right_arrival(t_right).wait_recv()
            from_left[t_right] += wsum[core, t_right]
            right_copy(from_left.at[t_right], t_right).start()

        @pl.when(chip == last)
        def _():
            left_copy(wsum.at[core, t_left], t_left).start()

        @pl.when((chip < last) & (last - chip <= step))
        def _():
            left_arrival(t_left).wait_recv()
            from_right[t_left] += wsum[core, t_left]
            left_copy(from_right.at[t_left], t_left).start()

    wgrad_ref[...] = wsum[core, chip]

    @pl.when(chip > 0)
    def _():
        right_arrival(chip).wait_recv()
        wgrad_ref[...] += from_left[chip]

    @pl.when(chip < last)
    def _():
        left_arrival(chip).wait_recv()
        wgrad_ref[...] += from_right[chip]

    each_peer(lambda j: anchor_copy(j).wait_send())
    each_peer(lambda j: ag_copy(j).wait_send())
    each_peer(lambda j: lhs_copy(j).wait_send())
    each_peer(lambda j: rhs_copy(j).wait_send())

    @pl.when(has_low)
    def _():
        face_copy(0).wait_send()
        hg_copy(0).wait_send()

    @pl.when(has_high)
    def _():
        face_copy(1).wait_send()
        hg_copy(1).wait_send()

    swap.wait_send()
    for step in range(chips - 1):
        t_right = last - step + chip
        t_left = step - (last - chip)

        @pl.when(chip <= step)
        def _():
            right_copy(from_left.at[t_right], t_right).wait_send()

        @pl.when(last - chip <= step)
        def _():
            left_copy(from_right.at[t_left], t_left).wait_send()


def body(
    cell_features,
    cotangent,
    query_weight,
    key_weight,
    value_weight,
    out_weight,
    anchor_index,
    face_cells,
    halo_count,
    neighbour_blocks,
):
    n_blk = lax.axis_size("blk")
    n_dom = lax.axis_size("dom")
    _, cells, width = cell_features.shape
    own_anchors = anchor_index.shape[1]
    rows = 4 * width // n_blk
    share = rows // n_dom
    chips = n_dom // 2
    picks = jnp.concatenate(
        [face_cells.reshape(1, 2 * BS)] + [anchor_index] * n_blk, axis=1
    )
    vmem = pl.BlockSpec(memory_space=pltpu.VMEM)
    smem = pl.BlockSpec(memory_space=pltpu.SMEM)
    dma = pltpu.SemaphoreType.DMA
    peers = [dma((n_blk,)) for _ in range(2)]
    sides = [dma((2,)) for _ in range(2)]
    mixed, cell_grad, weight_grads = pl.pallas_call(
        functools.partial(kernel, n_blk, n_dom),
        out_shape=(
            jax.ShapeDtypeStruct((cells, width), BF16),
            jax.ShapeDtypeStruct((cells, width), BF16),
            jax.ShapeDtypeStruct((share, width), F32),
        ),
        in_specs=[vmem] * 7 + [smem] * 2,
        out_specs=(vmem, vmem, vmem),
        scratch_shapes=[
            pltpu.VMEM((cells, width), BF16),
            pltpu.VMEM((cells, width), BF16),
            pltpu.VMEM((cells, width), BF16),
            pltpu.VMEM((cells, 2 * width), BF16),
            pltpu.VMEM((cells, 2 * BS + n_blk * own_anchors), BF16),
            pltpu.VMEM((2, BS, 2 * width), BF16),
            pltpu.VMEM((n_blk, own_anchors, 2 * width), BF16),
            pltpu.VMEM((2, BS, 2 * width), BF16),
            pltpu.VMEM((n_blk, own_anchors, 2 * width), BF16),
            pltpu.VMEM((n_blk, own_anchors, 2 * width), BF16),
            pltpu.VMEM((2, BS, 2 * width), BF16),
            pltpu.VMEM((2, BS, 2 * width), BF16),
            pltpu.VMEM((cells, 2 * width), F32),
            pltpu.VMEM((cells, width), F32),
            pltpu.VMEM((cells, width), F32),
            pltpu.VMEM((cells, width), BF16),
            pltpu.VMEM((3, cells, width), BF16),
            pltpu.VMEM((n_blk, cells, rows), BF16),
            pltpu.VMEM((n_blk, cells, width), BF16),
            pltpu.VMEM((2, chips, share, width), F32),
            pltpu.VMEM((chips, share, width), F32),
            pltpu.VMEM((chips, share, width), F32),
            pltpu.VMEM((chips, share, width), F32),
            *peers,
            *sides,
            *peers,
            *peers,
            *peers,
            *sides,
            dma((2,)),
            *[dma((chips,)) for _ in range(4)],
        ],
        compiler_params=pltpu.CompilerParams(
            collective_id=0, has_side_effects=True, vmem_limit_bytes=56 * 1024 * 1024
        ),
    )(
        cell_features[0],
        cotangent[0],
        query_weight,
        key_weight,
        value_weight,
        out_weight,
        picks,
        halo_count.reshape(1, 2),
        neighbour_blocks[0],
    )
    return mixed[None], cell_grad[None], weight_grads


def solution(mesh):
    return jax.shard_map(
        body,
        mesh=mesh,
        in_specs=(
            P("dom", "blk", None),
            P("dom", "blk", None),
            P(),
            P(),
            P(),
            P(),
            P("dom", "blk"),
            P("dom", "blk", None, None),
            P("dom", "blk", None),
            P("dom", "blk", None),
        ),
        out_specs=(P("dom", "blk", None), P("dom", "blk", None), P(("blk", "dom"), None)),
        check_vma=False,
    )
```

time: 366 us -> 88.2 us (0.24); the launches traced: 360 us -> 87.3 us
  waiting for transfers between devices: 131 us -> 0 us
  matrix products: 99.2 us -> 0 us
  Pallas kernels: 0 us -> 80.9 us
  local copies, waits for them, and re-layouts: 67.1 us -> 5.74 us
  other arithmetic: 28.5 us -> 0 us
  between operations: 14.5 us -> 0.65 us
  blocking collectives: 10.3 us -> 0 us
  starting transfers between devices: 8.83 us -> 0 us
    reduce_scatter x2 -> x0, waiting for transfers between devices: 131 us -> none  [the longest x1 131 us: body(): lax.psum_scatter(weight_term, ('blk', 'dom'), scatter_dimension=0, tiled=...]
    dot_general x85 -> x0, matrix products: 99.2 us -> none  [the longest x13 20 us: attend(): jnp.einsum('...qk,...ke->...qe', score_rounded, key_rows, preferred_eleme...]
    pallas_call x0 -> x1, Pallas kernels: none -> 80.9 us  [body(): pl.pallas_call(functools.partial(kernel, n_blk, n_dom), out_shape=(jax.Sh...]
    concatenate x6 -> x1, local copies, waits for them, and re-layouts: 16.9 us -> 1.45 us  [body(): jnp.concatenate([face_cells.reshape(1, 2 * BS)] + [anchor_index] * n_blk,...]
    slice x12 -> x0, local copies, waits for them, and re-layouts: 13.9 us -> none  [the longest x2 2.93 us: body(): queries = projected[:, :width]]
    concatenate x4 -> x0, other arithmetic: 11.3 us -> none  [the longest x1 7.27 us: body(): weight_term = jnp.concatenate([inner_term, out_term], 0)]
    all_gather x1 -> x0, blocking collectives: 10.3 us -> none  [body(): lax.all_gather(keyval_local[anchor_rows], 'blk', axis=0, tiled=True)]
    unnamed x66 -> x5, local copies, waits for them, and re-layouts: 13.4 us -> 4.29 us
  transfers between devices with their start and end apart: 6 -> 0, of which waited for: 1 -> 0; matrix products, arithmetic and copies ran while one was open for 46% -> 0% of each run, Pallas kernels for 0% -> 0%
where the time goes in v1:
time: 88.2 us; the launch traced here: 87.3 us
  Pallas kernels  80.9 us (92%)
  local copies, waits for them, and re-layouts  5.74 us (7%)
    pallas_call x1, Pallas kernels, body(): pl.pallas_call(functools.partial(kernel, n_blk, n_dom), out_shape=(jax.Sh...  80.9 us
    unnamed x5, local copies, waits for them, and re-layouts  4.29 us

profile of v1, /device:TPU:10, one launch (start us, length us, event | category | flops | bytes accessed | tf_op | source)
XLA Modules:
  0.0 87.3 jit_solution(17384561146136280793)
XLA Ops:
  0.6 1.4 %concatenate.3.idx_ref = s32[1,384]{1,0:T(1,128)} concatenate(s32[1,256]{1,0:T(1,128)} %bitcast.11, s32[1,32]{1,0:T(1,128)} %param.16, s32[1,32]{1,0:T(1,128)} %param.16, s32[1,32]{1,0:T(1,128)} %param.16, s32[1,32]{1,0:T(1,128)} %param.16), dimensions={1} | concatenate | bytes 3072 | tf_op jit(solution)/shard_map/concatenate | solution.py:520
  2.1 80.9 %shard_map.121 = (bf16[256,768]{1,0:T(8,128)(2,1)}, bf16[256,768]{1,0:T(8,128)(2,1)}, f32[96,768]{1,0:T(8,128)}) custom-call(bf16[256,768]{1,0:T(8,128)(2,1)} %bitcast.7, bf16[256,768]{1,0:T(8,128)(2,1)} %bitcast.8, bf16[768,768]{1,0:T(8,128)(2,1)} %wq_ref.1, bf16[768,768]{1,0:T(8,128)(2,1)} %wk_ref.1, bf16[768,768]{1,0:T(8,128)(2,1)} %wv_ref.1, ...), custom_call_target="tpu_custom_call" | custom-call | tf_op jit(solution)/shard_map/pallas_call | solution.py:528
  83.0 0.0 copy-start
  83.0 1.8 %copy.16 = bf16[1,256,768]{2,1,0:T(8,128)(2,1)} copy(bf16[1,256,768]{2,1,0:T(8,128)(2,1)} %bitcast.10) | data formatting | bytes 786432
  84.8 1.8 %copy.17 = bf16[1,256,768]{2,1,0:T(8,128)(2,1)} copy(bf16[1,256,768]{2,1,0:T(8,128)(2,1)} %bitcast.9) | data formatting | bytes 786432
  86.6 0.0 copy-done
  86.6 0.7 copy.18
Async XLA Ops:
  83.0 3.6 %copy-start = (f32[96,768]{1,0:T(8,128)S(1)}, f32[96,768]{1,0:T(8,128)}, u32[]{:S(2)}) copy-start(f32[96,768]{1,0:T(8,128)} %get-tuple-element.14) | copy-start | bytes 884740

commit v2 on v1

--- a/solution.py
+++ b/solution.py
@@ -12,6 +12,8 @@
 BS = 128
 EPSILON = 1e-06
 MASKED = -1e30
+LAG = 2
+PIECES = 3
 SCALING = 0.125
 MESH = pl.DeviceIdType.MESH
 F32 = jnp.float32
@@ -56,7 +58,8 @@
     wk_ref,
     wv_ref,
     wo_ref,
-    idx_ref,
+    anchor_ref,
+    face_ref,
     count_ref,
     near_ref,
     mixed_ref,
@@ -89,15 +92,16 @@
     anc_recv,
     face_send,
     face_recv,
-    lhs_send,
-    lhs_recv,
-    rhs_send,
-    rhs_recv,
+    early_send,
+    early_recv,
+    late_send,
+    late_recv,
     ag_send,
     ag_recv,
     hg_send,
     hg_recv,
-    core_sem,
+    core_send,
+    core_recv,
     right_send,
     right_recv,
     left_send,
@@ -105,7 +109,8 @@
 ):
     cells, width = x_ref.shape
     rows = lhs.shape[2]
-    share = wsum.shape[2]
+    share = wsum.shape[3]
+    piece = wsum.shape[4]
     chips = n_dom // 2
     pairs = width // PAIR
     blk = lax.axis_index("blk")
@@ -145,8 +150,18 @@
     kv_s[:, :width] = mm(normed[...], wk_ref[...]).astype(BF16)
     kv_s[:, width:] = mm(normed[...], wv_ref[...]).astype(BF16)
 
-    spots = lax.broadcasted_iota(jnp.int32, hot_s.shape, 0)
-    hot_s[...] = jnp.where(spots == idx_ref[...], 1.0, 0.0).astype(BF16)
+    own_anchors = anchors.shape[1]
+    anchor_count = n_blk * own_anchors
+    spots = lax.broadcasted_iota(jnp.int32, (cells, BS), 0)
+    for side in range(2):
+        hits = jnp.where(spots == face_ref[side : side + 1, :], 1.0, 0.0)
+        hot_s[:, side * BS : (side + 1) * BS] = hits.astype(BF16)
+    turn = lax.broadcasted_iota(jnp.int32, (own_anchors, anchor_count), 1) % own_anchors
+    same = lax.broadcasted_iota(jnp.int32, (own_anchors, anchor_count), 0) == turn
+    listed = jnp.broadcast_to(anchor_ref[...].astype(F32), (8, own_anchors)).astype(BF16)
+    repeated = mm(listed, jnp.where(same, 1.0, 0.0).astype(BF16))[:1]
+    places = lax.broadcasted_iota(jnp.int32, (cells, anchor_count), 0).astype(F32)
+    hot_s[:, 2 * BS :] = jnp.where(places == repeated, 1.0, 0.0).astype(BF16)
     picked = 2 * BS + anchors.shape[1]
     for part in range(2):
         columns = slice(part * width, (part + 1) * width)
@@ -185,48 +200,61 @@
     def weight_of(j):
         return (j * rows) // width, (j * rows) % width
 
-    def lhs_copy(j):
+    def early_copy(j):
         weight, start = weight_of(j)
-        source = normed if weight < 3 else att_b
-        return copy(
-            source.at[:, start : start + rows],
-            lhs.at[blk],
-            lhs_send.at[j],
-            lhs_recv.at[blk],
-            {"blk": j},
-        )
-
-    def rhs_copy(j):
-        weight, _ = weight_of(j)
-        source = grads.at[weight] if weight < 3 else dy_ref
-        return copy(source, rhs.at[blk], rhs_send.at[j], rhs_recv.at[blk], {"blk": j})
-
-    def lhs_own(j):
+        if weight < 3:
+            source, target = normed.at[:, start : start + rows], lhs.at[blk]
+        else:
+            source, target = dy_ref, rhs.at[blk]
+        return copy(source, target, early_send.at[j], early_recv.at[blk], {"blk": j})
+
+    def early_own(j):
         weight, start = weight_of(j)
-        source = normed if weight < 3 else att_b
-        lhs[j] = source[:, start : start + rows]
-
-    def rhs_own(j):
-        weight, _ = weight_of(j)
-        rhs[j] = grads[weight] if weight < 3 else dy_ref[...]
-
-    def send_lhs(wanted):
+        if weight < 3:
+            lhs[j] = normed[:, start : start + rows]
+        else:
+            rhs[j] = dy_ref[...]
+
+    def strip(h):
+        return pl.ds(pl.multiple_of(h * PAIR, PAIR), PAIR)
+
+    def late_copy(j, h):
+        weight, start = weight_of(j)
+        to = h - start // PAIR if weight == 3 else h
+        source = grads.at[weight, :, strip(h)] if weight < 3 else att_b.at[:, strip(h)]
+        target = rhs.at[blk, :, strip(to)] if weight < 3 else lhs.at[blk, :, strip(to)]
+        return copy(source, target, late_send.at[j, to], late_recv.at[blk, to], {"blk": j})
+
+    def send_late(weight, h):
         for j in range(n_blk):
-            if weight_of(j)[0] in wanted:
-                pl.when(blk != j)(functools.partial(lambda k: lhs_copy(k).start(), j))
-                pl.when(blk == j)(functools.partial(lhs_own, j))
-
-    def send_rhs(wanted):
-        for j in range(n_blk):
-            if weight_of(j)[0] in wanted:
-                pl.when(blk != j)(functools.partial(lambda k: rhs_copy(k).start(), j))
-                pl.when(blk == j)(functools.partial(rhs_own, j))
+            this, start = weight_of(j)
+            if this != weight:
+                continue
+
+            def send(j=j):
+                late_copy(j, h).start()
+
+            def own(j=j, start=start):
+                if weight < 3:
+                    rhs[j, :, strip(h)] = grads[weight, :, strip(h)]
+                else:
+                    lhs[j, :, strip(h - start // PAIR)] = att_b[:, strip(h)]
+
+            wanted = True
+            if weight == 3 and rows < width:
+                wanted = (h >= start // PAIR) & (h < (start + rows) // PAIR)
+            pl.when((blk != j) & wanted)(send)
+            pl.when((blk == j) & wanted)(own)
+
+    def send_early(j):
+        pl.when(blk != j)(lambda: early_copy(j).start())
+        pl.when(blk == j)(lambda: early_own(j))
 
     each_peer(lambda j: anchor_copy(j).start())
     pl.when(has_low)(lambda: face_copy(0).start())
     pl.when(has_high)(lambda: face_copy(1).start())
-    send_lhs((0, 1, 2))
-    send_rhs((3,))
+    for j in range(n_blk):
+        send_early(j)
 
     q_s[...] = mm(normed[...], wq_ref[...]).astype(BF16)
     g_s[...] = mm_nt(dy_ref[...], wo_ref[...]).astype(BF16)
@@ -255,8 +283,6 @@
         return jnp.where(keep, tensor[:half], tensor[half:])
 
     each_peer(lambda j: anchor_arrival(j).wait_recv())
-    anchor_count = n_blk * anchors.shape[1]
-
     def anchor_pair(h, carry):
         sl = pl.ds(pl.multiple_of(h * PAIR, PAIR), PAIR)
         vsl = pl.ds(pl.multiple_of(width + h * PAIR, PAIR), PAIR)
@@ -318,6 +344,41 @@
             listed = listed + inside
         live.append((listed * alive).astype(F32))
 
+    def hg_copy(side, h):
+        step = 2 * side - 1
+        return copy(
+            hg_out.at[side, h],
+            hg_in.at[1 - side, h],
+            hg_send.at[side, h],
+            hg_recv.at[1 - side, h],
+            {"dom": dom + step},
+        )
+
+    def hg_arrival(side, h):
+        step = 2 * side - 1
+        return copy(
+            hg_out.at[side, h],
+            hg_in.at[side, h],
+            hg_send.at[side, h],
+            hg_recv.at[side, h],
+            {"dom": dom + step},
+        )
+
+    def finish(h):
+        pl.when(has_low)(lambda: hg_arrival(0, h).wait_recv())
+        pl.when(has_high)(lambda: hg_arrival(1, h).wait_recv())
+        sl = strip(h)
+        vsl = pl.ds(pl.multiple_of(width + h * PAIR, PAIR), PAIR)
+        shares = jnp.concatenate([ag_in[:, :, sl], ag_in[:, :, vsl]], -1)
+        came = jnp.concatenate(
+            [hg_in[0, h], hg_in[1, h], shares.reshape(anchor_count, 2 * PAIR)], 0
+        )
+        total = near_s[h] + mm(hot_s[...], came)
+        grads[1, :, sl] = total[:, :PAIR].astype(BF16)
+        grads[2, :, sl] = total[:, PAIR:].astype(BF16)
+        send_late(1, h)
+        send_late(2, h)
+
     def near_pair(h, carry):
         sl = pl.ds(pl.multiple_of(h * PAIR, PAIR), PAIR)
         vsl = pl.ds(pl.multiple_of(width + h * PAIR, PAIR), PAIR)
@@ -329,173 +390,209 @@
             q2 = stacked(q_s[own, sl], SCALING)
             g2 = stacked(g_s[own, sl], 1.0)
             out, query_term, key_term, value_term = attend(q2, g2, keys, values, live[j])
-            att_f[own, sl] += unstacked(out)
-            qg_f[own, sl] += unstacked(query_term)
+            att_b[own, sl] = (att_f[own, sl] + unstacked(out)).astype(BF16)
+            grads[0, own, sl] = (qg_f[own, sl] + unstacked(query_term)).astype(BF16)
             key_sum = key_term if key_sum is None else key_sum + key_term
             value_sum = value_term if value_sum is None else value_sum + value_term
-        near_s[:, sl] = key_sum[:cells]
-        near_s[:, vsl] = value_sum[:cells]
+        near_s[h, :, :PAIR] = key_sum[:cells]
+        near_s[h, :, PAIR:] = value_sum[:cells]
         for side in range(2):
             part = slice(cells + side * BS, cells + (side + 1) * BS)
-            hg_out[side, :, sl] = key_sum[part].astype(BF16)
-            hg_out[side, :, vsl] = value_sum[part].astype(BF16)
+            hg_out[side, h, :, :PAIR] = key_sum[part].astype(BF16)
+            hg_out[side, h, :, PAIR:] = value_sum[part].astype(BF16)
+        pl.when(has_low)(lambda: hg_copy(0, h).start())
+        pl.when(has_high)(lambda: hg_copy(1, h).start())
+        send_late(3, h)
+        send_late(0, h)
+
+        @pl.when(h == LAG)
+        def _():
+            each_peer(lambda j: ag_arrival(j).wait_recv())
+
+        @pl.when(h >= LAG)
+        def _():
+            finish(h - LAG)
+
         return carry
 
     lax.fori_loop(0, pairs, near_pair, 0)
 
-    def hg_copy(side):
-        step = 2 * side - 1
+    def last_pair(h, carry):
+        finish(h)
+        return carry
+
+    lax.fori_loop(pairs - LAG, pairs, last_pair, 0)
+
+    is_out = blk * rows >= 3 * width
+
+    def late_arrival(j, h, buffer):
+        ref = buffer.at[j, :, strip(h)]
+        return copy(ref, ref, late_send.at[j, h], late_recv.at[j, h], {"blk": j})
+
+    def early_arrival(j, buffer):
+        ref = buffer.at[j]
+        return copy(ref, ref, early_send.at[j], early_recv.at[j], {"blk": j})
+
+    def arrivals(first_buffer, second_buffer, count, j):
+        early_arrival(j, first_buffer).wait_recv()
+
+        def one(h, carry):
+            late_arrival(j, h, second_buffer).wait_recv()
+            return carry
+
+        lax.fori_loop(0, count, one, 0)
+
+    @pl.when(is_out)
+    def _():
+        each_peer(functools.partial(arrivals, rhs, lhs, rows // PAIR))
+
+    @pl.when(jnp.logical_not(is_out))
+    def _():
+        each_peer(functools.partial(arrivals, lhs, rhs, pairs))
+
+    def swap(n):
         return copy(
-            hg_out.at[side],
-            hg_in.at[1 - side],
-            hg_send.at[side],
-            hg_recv.at[1 - side],
-            {"dom": dom + step},
-        )
-
-    def hg_arrival(side):
-        step = 2 * side - 1
+            wsum.at[n, 1 - core], wpart.at[n], core_send.at[n], core_recv.at[n], {"dom": mate}
+        )
+
+    left_all = lhs[...].reshape(n_blk * cells, rows)
+    for n in range(PIECES):
+        columns = slice(n * piece, (n + 1) * piece)
+        product = mm_tn(left_all, rhs[:, :, columns].reshape(n_blk * cells, piece))
+        for d in range(n_dom):
+            wsum[n, d % 2, d // 2] = product[d * share : (d + 1) * share]
+        swap(n).start()
+
+    def right_copy(source, n, t):
         return copy(
-            hg_out.at[side],
-            hg_in.at[side],
-            hg_send.at[side],
-            hg_recv.at[side],
-            {"dom": dom + step},
-        )
-
-    pl.when(has_low)(lambda: hg_copy(0).start())
-    pl.when(has_high)(lambda: hg_copy(1).start())
-    att_b[...] = att_f[...].astype(BF16)
-    grads[0] = qg_f[...].astype(BF16)
-    send_lhs((3,))
-    send_rhs((0,))
-
-    each_peer(lambda j: ag_arrival(j).wait_recv())
-    pl.when(has_low)(lambda: hg_arrival(0).wait_recv())
-    pl.when(has_high)(lambda: hg_arrival(1).wait_recv())
-
-    for part in (0, 1):
-        columns = slice(part * width, (part + 1) * width)
-        came = jnp.concatenate(
-            [
-                hg_in[0, :, columns],
-                hg_in[1, :, columns],
-                ag_in[:, :, columns].reshape(anchor_count, width),
-            ],
-            0,
-        )
-        grads[1 + part] = (near_s[:, columns] + mm(hot_s[...], came)).astype(BF16)
-        send_rhs((1 + part,))
-
-    mixed_ref[...] = (x_ref[...].astype(F32) + mm(att_b[...], wo_ref[...])).astype(BF16)
-    back = mm_nt(grads[0], wq_ref[...]) + mm_nt(grads[1], wk_ref[...])
-    back = back + mm_nt(grads[2], wv_ref[...])
-    x = x_ref[...].astype(F32)
-    inverse = lax.rsqrt(jnp.mean(x * x, axis=-1, keepdims=True) + EPSILON)
-    cube = inverse * inverse * inverse
-    pull = jnp.mean(back * x, axis=-1, keepdims=True)
-    cgrad_ref[...] = (dy_ref[...].astype(F32) + inverse * back - x * (cube * pull)).astype(BF16)
-
-    def operand_arrivals(j):
-        copy(lhs.at[j], lhs.at[j], lhs_send.at[j], lhs_recv.at[j], {"blk": j}).wait_recv()
-        copy(rhs.at[j], rhs.at[j], rhs_send.at[j], rhs_recv.at[j], {"blk": j}).wait_recv()
-
-    each_peer(operand_arrivals)
-    left_all = lhs[...].reshape(n_blk * cells, rows)
-    right_all = rhs[...].reshape(n_blk * cells, width)
-    product = mm_tn(left_all, right_all)
-    for d in range(n_dom):
-        wsum[d % 2, d // 2] = product[d * share : (d + 1) * share]
-
-    swap = copy(wsum.at[1 - core], wpart, core_sem.at[0], core_sem.at[1], {"dom": mate})
-    swap.start()
-    swap.wait_recv()
-    wsum[core] += wpart[...]
-
-    def right_copy(source, t):
+            source.at[n, t],
+            from_left.at[n, t],
+            right_send.at[n, t],
+            right_recv.at[n, t],
+            {"dom": dom + 2},
+        )
+
+    def left_copy(source, n, t):
         return copy(
-            source, from_left.at[t], right_send.at[t], right_recv.at[t], {"dom": dom + 2}
-        )
-
-    def left_copy(source, t):
-        return copy(
-            source, from_right.at[t], left_send.at[t], left_recv.at[t], {"dom": dom - 2}
-        )
-
-    def right_arrival(t):
-        return copy(
-            from_left.at[t], from_left.at[t], right_send.at[t], right_recv.at[t], {"dom": dom - 2}
-        )
-
-    def left_arrival(t):
-        return copy(
-            from_right.at[t], from_right.at[t], left_send.at[t], left_recv.at[t], {"dom": dom + 2}
-        )
+            source.at[n, t],
+            from_right.at[n, t],
+            left_send.at[n, t],
+            left_recv.at[n, t],
+            {"dom": dom - 2},
+        )
+
+    def right_arrival(n, t):
+        ref = from_left.at[n, t]
+        return copy(ref, ref, right_send.at[n, t], right_recv.at[n, t], {"dom": dom - 2})
+
+    def left_arrival(n, t):
+        ref = from_right.at[n, t]
+        return copy(ref, ref, left_send.at[n, t], left_recv.at[n, t], {"dom": dom + 2})
 
     last = chips - 1
     for step in range(chips - 1):
         t_right = last - step + chip
         t_left = step - (last - chip)
-
-        @pl.when(chip == 0)
+        for n in range(PIECES):
+            if step == 0:
+                swap(n).wait_recv()
+                wpart[n] += wsum[n, core]
+
+            @pl.when(chip == 0)
+            def _():
+                right_copy(wpart, n, t_right).start()
+
+            @pl.when((chip > 0) & (chip <= step))
+            def _():
+                right_arrival(n, t_right).wait_recv()
+                from_left[n, t_right] += wpart[n, t_right]
+                right_copy(from_left, n, t_right).start()
+
+            @pl.when(chip == last)
+            def _():
+                left_copy(wpart, n, t_left).start()
+
+            @pl.when((chip < last) & (last - chip <= step))
+            def _():
+                left_arrival(n, t_left).wait_recv()
+                from_right[n, t_left] += wpart[n, t_left]
+                left_copy(from_right, n, t_left).start()
+
+        if step > 0:
+            continue
+        mixed_ref[...] = (x_ref[...].astype(F32) + mm(att_b[...], wo_ref[...])).astype(BF16)
+        back = mm_nt(grads[0], wq_ref[...]) + mm_nt(grads[1], wk_ref[...])
+        back = back + mm_nt(grads[2], wv_ref[...])
+        x = x_ref[...].astype(F32)
+        inverse = lax.rsqrt(jnp.mean(x * x, axis=-1, keepdims=True) + EPSILON)
+        cube = inverse * inverse * inverse
+        pull = jnp.mean(back * x, axis=-1, keepdims=True)
+        cgrad_ref[...] = (dy_ref[...].astype(F32) + inverse * back - x * (cube * pull)).astype(BF16)
+
+    for n in range(PIECES):
+        columns = slice(n * piece, (n + 1) * piece)
+        wgrad_ref[:, columns] = wpart[n, chip]
+
+        @pl.when(chip > 0)
         def _():
-            right_copy(wsum.at[core, t_right], t_right).start()
-
-        @pl.when((chip > 0) & (chip <= step))
+            right_arrival(n, chip).wait_recv()
+            wgrad_ref[:, columns] += from_left[n, chip]
+
+        @pl.when(chip < last)
         def _():
-            right_arrival(t_right).wait_recv()
-            from_left[t_right] += wsum[core, t_right]
-            right_copy(from_left.at[t_right], t_right).start()
-
-        @pl.when(chip == last)
-        def _():
-            left_copy(wsum.at[core, t_left], t_left).start()
-
-        @pl.when((chip < last) & (last - chip <= step))
-        def _():
-            left_arrival(t_left).wait_recv()
-            from_right[t_left] += wsum[core, t_left]
-            left_copy(from_right.at[t_left], t_left).start()
-
-    wgrad_ref[...] = wsum[core, chip]
-
-    @pl.when(chip > 0)
-    def _():
-        right_arrival(chip).wait_recv()
-        wgrad_ref[...] += from_left[chip]
-
-    @pl.when(chip < last)
-    def _():
-        left_arrival(chip).wait_recv()
-        wgrad_ref[...] += from_right[chip]
+            left_arrival(n, chip).wait_recv()
+            wgrad_ref[:, columns] += from_right[n, chip]
 
     each_peer(lambda j: anchor_copy(j).wait_send())
     each_peer(lambda j: ag_copy(j).wait_send())
-    each_peer(lambda j: lhs_copy(j).wait_send())
-    each_peer(lambda j: rhs_copy(j).wait_send())
-
-    @pl.when(has_low)
-    def _():
-        face_copy(0).wait_send()
-        hg_copy(0).wait_send()
-
-    @pl.when(has_high)
-    def _():
-        face_copy(1).wait_send()
-        hg_copy(1).wait_send()
-
-    swap.wait_send()
-    for step in range(chips - 1):
-        t_right = last - step + chip
-        t_left = step - (last - chip)
-
-        @pl.when(chip <= step)
-        def _():
-            right_copy(from_left.at[t_right], t_right).wait_send()
-
-        @pl.when(last - chip <= step)
-        def _():
-            left_copy(from_right.at[t_left], t_left).wait_send()
+    each_peer(lambda j: early_copy(j).wait_send())
+
+    def late_sent(j):
+        weight, start = weight_of(j)
+        low, high = (0, pairs) if weight < 3 else (start // PAIR, (start + rows) // PAIR)
+
+        def one(h, carry):
+            late_copy(j, h).wait_send()
+            return carry
+
+        lax.fori_loop(low, high, one, 0)
+
+    each_peer(late_sent)
+
+    def hg_sent(side):
+        face_copy(side).wait_send()
+
+        def one(h, carry):
+            hg_copy(side, h).wait_send()
+            return carry
+
+        lax.fori_loop(0, pairs, one, 0)
+
+    pl.when(has_low)(lambda: hg_sent(0))
+    pl.when(has_high)(lambda: hg_sent(1))
+    for n in range(PIECES):
+        swap(n).wait_send()
+        for step in range(chips - 1):
+            t_right = last - step + chip
+            t_left = step - (last - chip)
+
+            @pl.when(chip <= step)
+            def _():
+                right_copy(from_left, n, t_right).wait_send()
+
+            @pl.when(last - chip <= step)
+            def _():
+                left_copy(from_right, n, t_left).wait_send()
+
+
+def deliver(*refs):
+    count = len(refs) // 3
+    sources, targets, sems = refs[:count], refs[count : 2 * count], refs[2 * count :]
+    copies = [pltpu.make_async_copy(*each) for each in zip(sources, targets, sems)]
+    for each in copies:
+        each.start()
+    for each in copies:
+        each.wait()
 
 
 def body(
@@ -517,14 +614,14 @@
     rows = 4 * width // n_blk
     share = rows // n_dom
     chips = n_dom // 2
-    picks = jnp.concatenate(
-        [face_cells.reshape(1, 2 * BS)] + [anchor_index] * n_blk, axis=1
-    )
+    piece = width // PIECES
+    pairs = width // PAIR
     vmem = pl.BlockSpec(memory_space=pltpu.VMEM)
     smem = pl.BlockSpec(memory_space=pltpu.SMEM)
     dma = pltpu.SemaphoreType.DMA
     peers = [dma((n_blk,)) for _ in range(2)]
     sides = [dma((2,)) for _ in range(2)]
+    chain = dma((PIECES, chips))
     mixed, cell_grad, weight_grads = pl.pallas_call(
         functools.partial(kernel, n_blk, n_dom),
         out_shape=(
@@ -532,7 +629,7 @@
             jax.ShapeDtypeStruct((cells, width), BF16),
             jax.ShapeDtypeStruct((share, width), F32),
         ),
-        in_specs=[vmem] * 7 + [smem] * 2,
+        in_specs=[vmem] * 8 + [smem] * 2,
         out_specs=(vmem, vmem, vmem),
         scratch_shapes=[
             pltpu.VMEM((cells, width), BF16),
@@ -545,27 +642,33 @@
             pltpu.VMEM((2, BS, 2 * width), BF16),
             pltpu.VMEM((n_blk, own_anchors, 2 * width), BF16),
             pltpu.VMEM((n_blk, own_anchors, 2 * width), BF16),
-            pltpu.VMEM((2, BS, 2 * width), BF16),
-            pltpu.VMEM((2, BS, 2 * width), BF16),
-            pltpu.VMEM((cells, 2 * width), F32),
+            pltpu.VMEM((2, pairs, BS, 2 * PAIR), BF16),
+            pltpu.VMEM((2, pairs, BS, 2 * PAIR), BF16),
+            pltpu.VMEM((pairs, cells, 2 * PAIR), F32),
             pltpu.VMEM((cells, width), F32),
             pltpu.VMEM((cells, width), F32),
             pltpu.VMEM((cells, width), BF16),
             pltpu.VMEM((3, cells, width), BF16),
             pltpu.VMEM((n_blk, cells, rows), BF16),
             pltpu.VMEM((n_blk, cells, width), BF16),
-            pltpu.VMEM((2, chips, share, width), F32),
-            pltpu.VMEM((chips, share, width), F32),
-            pltpu.VMEM((chips, share, width), F32),
-            pltpu.VMEM((chips, share, width), F32),
+            pltpu.VMEM((PIECES, 2, chips, share, piece), F32),
+            pltpu.VMEM((PIECES, chips, share, piece), F32),
+            pltpu.VMEM((PIECES, chips, share, piece), F32),
+            pltpu.VMEM((PIECES, chips, share, piece), F32),
             *peers,
             *sides,
             *peers,
+            dma((n_blk, pairs)),
+            dma((n_blk, pairs)),
             *peers,
-            *peers,
-            *sides,
-            dma((2,)),
-            *[dma((chips,)) for _ in range(4)],
+            dma((2, pairs)),
+            dma((2, pairs)),
+            dma((PIECES,)),
+            dma((PIECES,)),
+            chain,
+            chain,
+            chain,
+            chain,
         ],
         compiler_params=pltpu.CompilerParams(
             collective_id=0, has_side_effects=True, vmem_limit_bytes=56 * 1024 * 1024
@@ -577,10 +680,20 @@
         key_weight,
         value_weight,
         out_weight,
-        picks,
+        anchor_index,
+        face_cells.reshape(2, BS),
         halo_count.reshape(1, 2),
         neighbour_blocks[0],
     )
+    anywhere = pl.BlockSpec(memory_space=pl.ANY)
+    results = (mixed, cell_grad, weight_grads)
+    mixed, cell_grad, weight_grads = pl.pallas_call(
+        deliver,
+        out_shape=tuple(jax.ShapeDtypeStruct(each.shape, each.dtype) for each in results),
+        in_specs=[anywhere] * 3,
+        out_specs=(anywhere,) * 3,
+        scratch_shapes=[dma, dma, dma],
+    )(*results)
     return mixed[None], cell_grad[None], weight_grads
 
 

time: 88.2 us -> 113 us (1.28)
  Pallas kernels: 80.9 us -> 112 us
  local copies, waits for them, and re-layouts: 5.74 us -> 0 us
    pallas_call x0 -> x1, Pallas kernels: none -> 33.9 us  [body(): pl.pallas_call(deliver, out_shape=tuple((jax.ShapeDtypeStruct(each.shape,...]
    unnamed x5 -> x0, local copies, waits for them, and re-layouts: 4.29 us -> none
    pallas_call x1, Pallas kernels: 80.9 us -> 78.1 us  [body(): pl.pallas_call(functools.partial(kernel, n_blk, n_dom), out_shape=(jax.Sh...]
    concatenate x1 -> x0, local copies, waits for them, and re-layouts: 1.45 us -> none  [body(): jnp.concatenate([face_cells.reshape(1, 2 * BS)] + [anchor_index] * n_blk,...]
where the time goes in v2:
time: 113 us
  Pallas kernels  112 us (99%)
    pallas_call x1, Pallas kernels, body(): pl.pallas_call(functools.partial(kernel, n_blk, n_dom), out_shape=(jax.Sh...  78.1 us
    pallas_call x1, Pallas kernels, body(): pl.pallas_call(deliver, out_shape=tuple((jax.ShapeDtypeStruct(each.shape,...  33.9 us

profile of v2, /device:TPU:10, one launch (start us, length us, event | category | flops | bytes accessed | tf_op | source)
XLA Modules:
  0.0 112.7 jit_solution(17090420099682220130)
XLA Ops:
  0.6 78.1 %shard_map.121 = (bf16[256,768]{1,0:T(8,128)(2,1)}, bf16[256,768]{1,0:T(8,128)(2,1)}, f32[96,768]{1,0:T(8,128)}) custom-call(bf16[256,768]{1,0:T(8,128)(2,1)} %bitcast.7, bf16[256,768]{1,0:T(8,128)(2,1)} %bitcast.8, bf16[768,768]{1,0:T(8,128)(2,1)} %wq_ref.1, bf16[768,768]{1,0:T(8,128)(2,1)} %wk_ref.1, bf16[768,768]{1,0:T(8,128)(2,1)} %wv_ref.1, ...), custom_call_target="tpu_custom_call" | custom-call | tf_op jit(solution)/shard_map/pallas_call | solution.py:625
  78.8 33.9 %shard_map.122 = (bf16[256,768]{1,0:T(8,128)(2,1)}, bf16[256,768]{1,0:T(8,128)(2,1)}, f32[96,768]{1,0:T(8,128)}) custom-call(bf16[256,768]{1,0:T(8,128)(2,1)} %get-tuple-element.9.refs_0_, bf16[256,768]{1,0:T(8,128)(2,1)} %get-tuple-element.10.refs_1_, f32[96,768]{1,0:T(8,128)} %get-tuple-element.11.refs_2_), custom_call_target="tpu_custom_call" | custom-call | tf_op jit(solution)/shard_map/pallas_call | solution.py:690

commit v3 on v2

--- a/solution.py
+++ b/solution.py
@@ -84,6 +84,7 @@
     grads,
     lhs,
     rhs,
+    lhs_t,
     wsum,
     wpart,
     from_left,
@@ -417,11 +418,21 @@
 
     lax.fori_loop(0, pairs, near_pair, 0)
 
-    def last_pair(h, carry):
+    for h in range(pairs - LAG, pairs):
         finish(h)
-        return carry
-
-    lax.fori_loop(pairs - LAG, pairs, last_pair, 0)
+        if h == pairs - LAG:
+            mixed = x_ref[...].astype(F32) + mm(att_b[...], wo_ref[...])
+            mixed_ref[...] = mixed.astype(BF16)
+
+    def cell_gradient():
+        back = mm_nt(grads[0], wq_ref[...]) + mm_nt(grads[1], wk_ref[...])
+        back = back + mm_nt(grads[2], wv_ref[...])
+        x = x_ref[...].astype(F32)
+        inverse = lax.rsqrt(jnp.mean(x * x, axis=-1, keepdims=True) + EPSILON)
+        cube = inverse * inverse * inverse
+        pull = jnp.mean(back * x, axis=-1, keepdims=True)
+        total = dy_ref[...].astype(F32) + inverse * back - x * (cube * pull)
+        cgrad_ref[...] = total.astype(BF16)
 
     is_out = blk * rows >= 3 * width
 
@@ -433,32 +444,39 @@
         ref = buffer.at[j]
         return copy(ref, ref, early_send.at[j], early_recv.at[j], {"blk": j})
 
-    def arrivals(first_buffer, second_buffer, count, j):
-        early_arrival(j, first_buffer).wait_recv()
-
+    def late_arrivals(buffer, low, high, j):
         def one(h, carry):
-            late_arrival(j, h, second_buffer).wait_recv()
+            late_arrival(j, h, buffer).wait_recv()
             return carry
 
-        lax.fori_loop(0, count, one, 0)
+        lax.fori_loop(low, high, one, 0)
 
     @pl.when(is_out)
     def _():
-        each_peer(functools.partial(arrivals, rhs, lhs, rows // PAIR))
+        each_peer(lambda j: early_arrival(j, rhs).wait_recv())
+        each_peer(functools.partial(late_arrivals, lhs, 0, rows // PAIR))
 
     @pl.when(jnp.logical_not(is_out))
     def _():
-        each_peer(functools.partial(arrivals, lhs, rhs, pairs))
+        each_peer(lambda j: early_arrival(j, lhs).wait_recv())
+
+    for j in range(n_blk):
+        lhs_t[:, j * cells : (j + 1) * cells] = lhs[j].T
 
     def swap(n):
         return copy(
             wsum.at[n, 1 - core], wpart.at[n], core_send.at[n], core_recv.at[n], {"dom": mate}
         )
 
-    left_all = lhs[...].reshape(n_blk * cells, rows)
-    for n in range(PIECES):
+    strips = piece // PAIR
+
+    def weight_piece(n):
+        @pl.when(jnp.logical_not(is_out))
+        def _():
+            each_peer(functools.partial(late_arrivals, rhs, n * strips, (n + 1) * strips))
+
         columns = slice(n * piece, (n + 1) * piece)
-        product = mm_tn(left_all, rhs[:, :, columns].reshape(n_blk * cells, piece))
+        product = mm(lhs_t[...], rhs[:, :, columns].reshape(n_blk * cells, piece))
         for d in range(n_dom):
             wsum[n, d % 2, d // 2] = product[d * share : (d + 1) * share]
         swap(n).start()
@@ -490,44 +508,42 @@
         return copy(ref, ref, left_send.at[n, t], left_recv.at[n, t], {"dom": dom + 2})
 
     last = chips - 1
-    for step in range(chips - 1):
+
+    def chain(n, step):
         t_right = last - step + chip
         t_left = step - (last - chip)
-        for n in range(PIECES):
-            if step == 0:
-                swap(n).wait_recv()
-                wpart[n] += wsum[n, core]
-
-            @pl.when(chip == 0)
-            def _():
-                right_copy(wpart, n, t_right).start()
-
-            @pl.when((chip > 0) & (chip <= step))
-            def _():
-                right_arrival(n, t_right).wait_recv()
-                from_left[n, t_right] += wpart[n, t_right]
-                right_copy(from_left, n, t_right).start()
-
-            @pl.when(chip == last)
-            def _():
-                left_copy(wpart, n, t_left).start()
-
-            @pl.when((chip < last) & (last - chip <= step))
-            def _():
-                left_arrival(n, t_left).wait_recv()
-                from_right[n, t_left] += wpart[n, t_left]
-                left_copy(from_right, n, t_left).start()
-
-        if step > 0:
-            continue
-        mixed_ref[...] = (x_ref[...].astype(F32) + mm(att_b[...], wo_ref[...])).astype(BF16)
-        back = mm_nt(grads[0], wq_ref[...]) + mm_nt(grads[1], wk_ref[...])
-        back = back + mm_nt(grads[2], wv_ref[...])
-        x = x_ref[...].astype(F32)
-        inverse = lax.rsqrt(jnp.mean(x * x, axis=-1, keepdims=True) + EPSILON)
-        cube = inverse * inverse * inverse
-        pull = jnp.mean(back * x, axis=-1, keepdims=True)
-        cgrad_ref[...] = (dy_ref[...].astype(F32) + inverse * back - x * (cube * pull)).astype(BF16)
+        if step == 0:
+            swap(n).wait_recv()
+            wpart[n] += wsum[n, core]
+
+        @pl.when(chip == 0)
+        def _():
+            right_copy(wpart, n, t_right).start()
+
+        @pl.when((chip > 0) & (chip <= step))
+        def _():
+            right_arrival(n, t_right).wait_recv()
+            from_left[n, t_right] += wpart[n, t_right]
+            right_copy(from_left, n, t_right).start()
+
+        @pl.when(chip == last)
+        def _():
+            left_copy(wpart, n, t_left).start()
+
+        @pl.when((chip < last) & (last - chip <= step))
+        def _():
+            left_arrival(n, t_left).wait_recv()
+            from_right[n, t_left] += wpart[n, t_left]
+            left_copy(from_right, n, t_left).start()
+
+    for wave in range(PIECES + chips - 2):
+        if wave < PIECES:
+            weight_piece(wave)
+        if wave == PIECES - 1:
+            cell_gradient()
+        for n in range(min(wave, PIECES - 1), -1, -1):
+            if wave - n < chips - 1:
+                chain(n, wave - n)
 
     for n in range(PIECES):
         columns = slice(n * piece, (n + 1) * piece)
@@ -586,13 +602,9 @@
 
 
 def deliver(*refs):
-    count = len(refs) // 3
-    sources, targets, sems = refs[:count], refs[count : 2 * count], refs[2 * count :]
-    copies = [pltpu.make_async_copy(*each) for each in zip(sources, targets, sems)]
-    for each in copies:
-        each.start()
-    for each in copies:
-        each.wait()
+    count = len(refs) // 2
+    for source, target in zip(refs[:count], refs[count:]):
+        target[...] = source[...]
 
 
 def body(
@@ -651,6 +663,7 @@
             pltpu.VMEM((3, cells, width), BF16),
             pltpu.VMEM((n_blk, cells, rows), BF16),
             pltpu.VMEM((n_blk, cells, width), BF16),
+            pltpu.VMEM((rows, n_blk * cells), BF16),
             pltpu.VMEM((PIECES, 2, chips, share, piece), F32),
             pltpu.VMEM((PIECES, chips, share, piece), F32),
             pltpu.VMEM((PIECES, chips, share, piece), F32),
@@ -685,14 +698,12 @@
         halo_count.reshape(1, 2),
         neighbour_blocks[0],
     )
-    anywhere = pl.BlockSpec(memory_space=pl.ANY)
     results = (mixed, cell_grad, weight_grads)
     mixed, cell_grad, weight_grads = pl.pallas_call(
         deliver,
         out_shape=tuple(jax.ShapeDtypeStruct(each.shape, each.dtype) for each in results),
-        in_specs=[anywhere] * 3,
-        out_specs=(anywhere,) * 3,
-        scratch_shapes=[dma, dma, dma],
+        in_specs=[vmem] * 3,
+        out_specs=(vmem,) * 3,
     )(*results)
     return mixed[None], cell_grad[None], weight_grads
 

time: 113 us -> 77.9 us (0.69)
  Pallas kernels: 112 us -> 76.3 us
    pallas_call x1, Pallas kernels: 33.9 us -> 2.2 us  [body(): pl.pallas_call(deliver, out_shape=tuple((jax.ShapeDtypeStruct(each.shape,...]
    pallas_call x1, Pallas kernels: 78.1 us -> 74.1 us  [body(): pl.pallas_call(functools.partial(kernel, n_blk, n_dom), out_shape=(jax.Sh...]
where the time goes in v3:
time: 77.9 us; the launch traced here: 76.9 us
  Pallas kernels  76.3 us (98%)
    pallas_call x1, Pallas kernels, body(): pl.pallas_call(functools.partial(kernel, n_blk, n_dom), out_shape=(jax.Sh...  74.1 us
    pallas_call x1, Pallas kernels, body(): pl.pallas_call(deliver, out_shape=tuple((jax.ShapeDtypeStruct(each.shape,...  2.2 us

profile of v3, /device:TPU:10, one launch (start us, length us, event | category | flops | bytes accessed | tf_op | source)
XLA Modules:
  0.0 76.9 jit_solution(15455020062237329128)
XLA Ops:
  0.6 74.1 %shard_map.121 = (bf16[256,768]{1,0:T(8,128)(2,1)}, bf16[256,768]{1,0:T(8,128)(2,1)}, f32[96,768]{1,0:T(8,128)}) custom-call(bf16[256,768]{1,0:T(8,128)(2,1)} %bitcast.7, bf16[256,768]{1,0:T(8,128)(2,1)} %bitcast.8, bf16[768,768]{1,0:T(8,128)(2,1)} %wq_ref.1, bf16[768,768]{1,0:T(8,128)(2,1)} %wk_ref.1, bf16[768,768]{1,0:T(8,128)(2,1)} %wv_ref.1, ...), custom_call_target="tpu_custom_call" | custom-call | tf_op jit(solution)/shard_map/pallas_call | solution.py:637
  74.7 2.2 %shard_map.122 = (bf16[256,768]{1,0:T(8,128)(2,1)}, bf16[256,768]{1,0:T(8,128)(2,1)}, f32[96,768]{1,0:T(8,128)}) custom-call(bf16[256,768]{1,0:T(8,128)(2,1)} %get-tuple-element.9.refs_0_, bf16[256,768]{1,0:T(8,128)(2,1)} %get-tuple-element.10.refs_1_, f32[96,768]{1,0:T(8,128)} %get-tuple-element.11.refs_2_), custom_call_target="tpu_custom_call" | custom-call | tf_op jit(solution)/shard_map/pallas_call | solution.py:702

commit v4 on v3

--- a/solution.py
+++ b/solution.py
@@ -12,7 +12,7 @@
 BS = 128
 EPSILON = 1e-06
 MASKED = -1e30
-LAG = 2
+LAG = 3
 PIECES = 3
 SCALING = 0.125
 MESH = pl.DeviceIdType.MESH
@@ -44,8 +44,8 @@
     score_grad = prob * (prob_grad - jnp.sum(prob * prob_grad, axis=-1, keepdims=True))
     score_b = score_grad.astype(BF16)
     query_term = mm(score_b, keys) * SCALING
-    key_term = mm_tn(score_b, q2)
-    value_term = mm_tn(prob_b, g2)
+    key_term = mm_tn(q2, score_b)
+    value_term = mm_tn(g2, prob_b)
     return out, query_term, key_term, value_term
 
 
@@ -294,11 +294,11 @@
         out, query_term, key_term, value_term = attend(q2, g2, keys, values, None)
         att_f[:, sl] = unstacked(out)
         qg_f[:, sl] = unstacked(query_term)
-        ag_out[:, :, sl] = key_term.astype(BF16).reshape(n_blk, -1, PAIR)
-        ag_out[:, :, vsl] = value_term.astype(BF16).reshape(n_blk, -1, PAIR)
+        ag_out[:, :, sl] = key_term.T.astype(BF16).reshape(n_blk, -1, PAIR)
+        ag_out[:, :, vsl] = value_term.T.astype(BF16).reshape(n_blk, -1, PAIR)
         return carry
 
-    lax.fori_loop(0, pairs, anchor_pair, 0)
+    lax.fori_loop(0, pairs, anchor_pair, 0, unroll=2)
 
     def ag_copy(j):
         return copy(ag_out.at[j], ag_in.at[blk], ag_send.at[j], ag_recv.at[blk], {"blk": j})
@@ -395,6 +395,8 @@
             grads[0, own, sl] = (qg_f[own, sl] + unstacked(query_term)).astype(BF16)
             key_sum = key_term if key_sum is None else key_sum + key_term
             value_sum = value_term if value_sum is None else value_sum + value_term
+        key_sum = key_sum.T
+        value_sum = value_sum.T
         near_s[h, :, :PAIR] = key_sum[:cells]
         near_s[h, :, PAIR:] = value_sum[:cells]
         for side in range(2):

time: 77.9 us -> 78.9 us (1.013); the launches traced: 76.9 us -> 78.7 us
  Pallas kernels: 76.3 us -> 78.1 us
    pallas_call x1, Pallas kernels: 74.1 us -> 75.9 us  [body(): pl.pallas_call(functools.partial(kernel, n_blk, n_dom), out_shape=(jax.Sh...]
where the time goes in v4:
time: 78.9 us; the launch traced here: 78.7 us
  Pallas kernels  78.1 us (99%)
    pallas_call x1, Pallas kernels, body(): pl.pallas_call(functools.partial(kernel, n_blk, n_dom), out_shape=(jax.Sh...  75.9 us
    pallas_call x1, Pallas kernels, body(): pl.pallas_call(deliver, out_shape=tuple((jax.ShapeDtypeStruct(each.shape,...  2.2 us

profile of v4, /device:TPU:10, one launch (start us, length us, event | category | flops | bytes accessed | tf_op | source)
XLA Modules:
  0.0 78.7 jit_solution(786939228233454385)
XLA Ops:
  0.6 75.9 %shard_map.121 = (bf16[256,768]{1,0:T(8,128)(2,1)}, bf16[256,768]{1,0:T(8,128)(2,1)}, f32[96,768]{1,0:T(8,128)}) custom-call(bf16[256,768]{1,0:T(8,128)(2,1)} %bitcast.7, bf16[256,768]{1,0:T(8,128)(2,1)} %bitcast.8, bf16[768,768]{1,0:T(8,128)(2,1)} %wq_ref.1, bf16[768,768]{1,0:T(8,128)(2,1)} %wk_ref.1, bf16[768,768]{1,0:T(8,128)(2,1)} %wv_ref.1, ...), custom_call_target="tpu_custom_call" | custom-call | tf_op jit(solution)/shard_map/pallas_call | solution.py:639
  76.5 2.2 %shard_map.122 = (bf16[256,768]{1,0:T(8,128)(2,1)}, bf16[256,768]{1,0:T(8,128)(2,1)}, f32[96,768]{1,0:T(8,128)}) custom-call(bf16[256,768]{1,0:T(8,128)(2,1)} %get-tuple-element.9.refs_0_, bf16[256,768]{1,0:T(8,128)(2,1)} %get-tuple-element.10.refs_1_, f32[96,768]{1,0:T(8,128)} %get-tuple-element.11.refs_2_), custom_call_target="tpu_custom_call" | custom-call | tf_op jit(solution)/shard_map/pallas_call | solution.py:704
